TPU v7x, 512 devices: a whole 4x4x16 slice. The times are simulated.
512 devices in a mesh: tensor: 16 (over x, z_hi), feature: 8 (over y, core), dp: 4 (over z_lo).
Axes of the slice: x: 4, y: 4, z: 16 (z_hi: 4, z_lo: 4; z = z_hi * 4 + z_lo), core: 2. Of those that a mesh axis runs over, the one named last changes fastest.
Arguments:
- mlp_input: bfloat16 [64, 4096], P(None, ('feature', 'dp')), may hold values from -6 to 6
- gate_weight: bfloat16 [4096, 28672], P(('feature', 'dp'), 'tensor'), may hold values from -0.09375 to 0.09375
- up_weight: bfloat16 [4096, 28672], P(('feature', 'dp'), 'tensor'), may hold values from -0.09375 to 0.09375
- down_weight: bfloat16 [28672, 4096], P('tensor', ('feature', 'dp')), may hold values from -0.03125 to 0.03125
- down_encoder: bfloat16 [65536, 4096], P('tensor', ('feature', 'dp')), may hold values from -6 to 6
- feature_ids: int32 [32], replicated, may hold values from 0 to 65535
- up_decoder: bfloat16 [131072, 4096], P('tensor', ('feature', 'dp')), may hold values from -0.09375 to 0.09375
- latent_ids: int32 [64, 64], replicated, may hold values from 0 to 131071, as said below
- latent_acts: float32 [64, 64], P('dp', 'tensor'), may hold values from 0.5 to 4
Outputs:
- attribution: float32 [32, 64, 64], P('feature', 'dp', 'tensor')
Inputs may be any that keep to these rules, and one draw needn't show every extreme that they name: `latent_ids`: the 64 latents of one token are distinct.
All inputs are finite; a program needn't handle non-finite values.
Results may differ from a plain program's by a relative error of at most 0.0029.
Values may be sent and summed in bfloat16 or wider, within the bound.
No kernel may reach another device: no remote copies, remote signals or barrier semaphores. Data moves between devices by JAX's collectives and lax.ppermute only.
A program may use at most 64 MiB of HBM per device.

v0:
```python
import math
import jax
import jax.numpy as jnp
from jax import lax
from jax.sharding import PartitionSpec as P


def factors(gate_pre, up_pre):
    sigmoid_gate = jax.nn.sigmoid(gate_pre)
    gate_factor = up_pre * sigmoid_gate * (1.0 + gate_pre * (1.0 - sigmoid_gate))
    up_factor = gate_pre * sigmoid_gate
    return (gate_factor, up_factor)


def arrange_blocks(partial_value, count_tensor, count_feature, count_data):
    features = partial_value.shape[0]
    tokens = partial_value.shape[1]
    slots = partial_value.shape[2]
    arranged = partial_value.reshape(
        count_feature,
        features // count_feature,
        count_data,
        tokens // count_data,
        count_tensor,
        slots // count_tensor,
    )
    arranged = arranged.transpose(4, 0, 2, 1, 3, 5)
    return arranged.reshape(
        count_tensor * count_feature * count_data,
        features // count_feature,
        tokens // count_data,
        slots // count_tensor,
    )


def on_device(
    mlp_input,
    gate_weight,
    up_weight,
    down_weight,
    down_encoder,
    feature_ids,
    up_decoder,
    latent_ids,
    latent_acts,
):
    contract = (((1,), (1,)), ((), ()))
    tensor_rank = lax.axis_index("tensor")
    tokens = mlp_input.shape[0]
    dblk = gate_weight.shape[0]
    ffblk = gate_weight.shape[1]
    features = feature_ids.shape[0]
    count_tensor = lax.axis_size("tensor")
    count_feature = lax.axis_size("feature")
    count_data = lax.axis_size("dp")
    enc_rows = down_encoder.shape[0]
    local_ids = feature_ids - tensor_rank * enc_rows
    picker = (local_ids[:, None] == jnp.arange(enc_rows, dtype=jnp.int32)[None, :]).astype(
        jnp.bfloat16
    )
    chosen = lax.psum(jnp.dot(picker, down_encoder, preferred_element_type=jnp.float32), "tensor")
    cotangent = chosen.astype(jnp.bfloat16)
    neuron_part = lax.dot_general(
        cotangent, down_weight, contract, preferred_element_type=jnp.float32
    )
    gate_part = jnp.dot(mlp_input, gate_weight, preferred_element_type=jnp.float32)
    up_part = jnp.dot(mlp_input, up_weight, preferred_element_type=jnp.float32)
    gate_pre, up_pre, neuron_grad = lax.psum((gate_part, up_part, neuron_part), ("feature", "dp"))
    gate_factor, up_factor = factors(gate_pre, up_pre)
    per_block = math.gcd(features, 8)
    grouped_rows = neuron_grad.reshape(features // per_block, per_block, ffblk)

    def feature_block(grad_rows):
        grad_gate = (
            (grad_rows[:, None, :] * gate_factor[None])
            .astype(jnp.bfloat16)
            .reshape(per_block * tokens, ffblk)
        )
        grad_up = (
            (grad_rows[:, None, :] * up_factor[None])
            .astype(jnp.bfloat16)
            .reshape(per_block * tokens, ffblk)
        )
        width_grad = lax.dot_general(
            grad_gate, gate_weight, contract, preferred_element_type=jnp.float32
        )
        width_grad = width_grad + lax.dot_general(
            grad_up, up_weight, contract, preferred_element_type=jnp.float32
        )
        return width_grad.reshape(per_block, tokens, dblk)

    width_part = lax.map(feature_block, grouped_rows).reshape(features, tokens, dblk)
    dec_rows = up_decoder.shape[0]
    local_latents = latent_ids - tensor_rank * dec_rows
    owner_mask = jnp.logical_and(local_latents >= 0, local_latents < dec_rows)
    picked = jnp.take(up_decoder, jnp.clip(local_latents, 0, dec_rows - 1), axis=0)
    picked = picked * owner_mask[:, :, None].astype(jnp.bfloat16)
    width_full = lax.psum(width_part, "tensor")
    partial_value = jnp.einsum(
        "ftd,tkd->ftk", width_full, picked.astype(jnp.float32), precision=lax.Precision.HIGHEST
    )
    arranged = arrange_blocks(partial_value, count_tensor, count_feature, count_data)
    own_block = lax.psum_scatter(
        arranged, ("tensor", "feature", "dp"), scatter_dimension=0, tiled=True
    )[0]
    return own_block * latent_acts[None, :, :]


def solution(mesh):
    in_specs = (
        P(None, ("feature", "dp")),
        P(("feature", "dp"), "tensor"),
        P(("feature", "dp"), "tensor"),
        P("tensor", ("feature", "dp")),
        P("tensor", ("feature", "dp")),
        P(),
        P("tensor", ("feature", "dp")),
        P(),
        P("dp", "tensor"),
    )
    out_specs = P("feature", "dp", "tensor")
    return jax.shard_map(
        on_device, mesh=mesh, in_specs=in_specs, out_specs=out_specs, check_vma=False
    )
```

profile of v0, /device:TPU:2, one launch (start us, length us, event | category | flops | bytes accessed | tf_op | source)
XLA Modules:
  0.0 1137.1 jit_solution(10292003025647488974)
XLA Ops:
  6.5 0.0 copy-start
  6.5 0.0 copy-start.1
  6.5 0.0 copy-start.3
  6.5 0.0 all-reduce.10.cloned.1.call-start
  6.6 0.8 broadcast_subtract_fusion
  7.4 1.6 fusion.5
  9.0 99.8 %psum.35 = bf16[32,128]{1,0:T(8,128)(2,1)S(1)} all-reduce(f32[32,128]{1,0:T(8,128)S(1)} %fusion.5), channel_id=1, replica_groups=mesh['tensor'=16,'feature'=8,'dp'=4] {'tensor'}, use_global_device_ids=true, to_apply=%region_0.0 | all-reduce | flops 4096 | bytes 24576 | tf_op jit(solution)/shard_map/psum | solution.py:61
  108.8 2.0 fusion.12
  110.8 0.0 copy-done.1
  110.8 1.7 fusion.13
  112.5 0.0 copy-done.3
  112.5 1.0 convolution_bitcast_fusion
  113.5 0.0 all-reduce.10.cloned.1.call-update
  113.5 0.0 all-reduce.6.cloned.1.call-start
  113.5 283.3 %all-reduce.10.cloned.1.call-done = (f32[4,8,1792]{2,1,0:T(8,128)}, f32[64,1792]{1,0:T(8,128)}, f32[64,1792]{1,0:T(8,128)}) async-done(((f32[4,8,1792]{2,1,0:T(8,128)}, f32[64,1792]{1,0:T(8,128)}, f32[64,1792]{1,0:T(8,128)}), (f32[4,8,1792]{2,1,0:T(8,128)}, f32[64,1792]{1,0:T(8,128)}, f32[64,1792]{1,0:T(8,128)})) %all-reduce.10.cloned.1.call-update) | async-done | bytes 1146896 | tf_op jit(solution)/shard_map/psum | solution.py:68
  396.9 1.4 fusion.6
  398.2 0.0 copy-start.4
  398.2 16.5 %while.10 = (s32[]{:T(128)}, f32[4,8,64,128]{3,1,0,2:T(8,128)}, f32[4,8,1792]{2,1,0:T(8,128)}, f32[64,1792]{1,0:T(8,128)S(1)}, bf16[128,1792]{1,0:T(8,128)(2,1)S...) while((s32[]{:T(128)}, f32[4,8,64,128]{3,1,0,2:T(8,128)}, f32[4,8,1792]{2,1,0:T(8,128)}, ...), condition=%wide.region_5.6_spmd, body=%wide.region_4.5_spmd.sunk | while | flops 473497600 | bytes 12493429 | solution.py:92
  398.3 0.8 dynamic-slice_bitcast_fusion.3
  399.1 0.7 multiply_convert_fusion.3
  399.8 0.0 copy-start.2
  399.8 0.6 fusion.35
  400.5 0.4 copy-done.2
  400.8 0.6 convolution_add_fusion.2
  401.5 0.9 copy_dynamic-update-slice_fusion.2
  402.4 0.8 dynamic-slice_bitcast_fusion.3
  403.2 0.7 multiply_convert_fusion.3
  403.9 0.0 copy-start.2
  403.9 0.6 fusion.35
  404.6 0.4 copy-done.2
  404.9 0.6 convolution_add_fusion.2
  405.6 0.9 copy_dynamic-update-slice_fusion.2
  406.5 0.8 dynamic-slice_bitcast_fusion.3
  407.3 0.7 multiply_convert_fusion.3
  408.0 0.0 copy-start.2
  408.0 0.6 fusion.35
  408.7 0.4 copy-done.2
  409.0 0.6 convolution_add_fusion.2
  409.7 0.9 copy_dynamic-update-slice_fusion.2
  410.6 0.8 dynamic-slice_bitcast_fusion.3
  411.5 0.7 multiply_convert_fusion.3
  412.2 0.0 copy-start.2
  412.2 0.6 fusion.35
  412.8 0.4 copy-done.2
  413.2 0.6 convolution_add_fusion.2
  413.9 0.9 copy_dynamic-update-slice_fusion.2
  414.8 0.0 all-reduce.6.cloned.1.call-update
  414.8 0.0 all-reduce.8.cloned.1.call-start
  414.8 0.0 copy-done.4
  414.9 0.1 reshape.43
  415.0 0.0 copy-done
  415.0 12.1 %gather_fusion = bf16[4096,128]{1,0:T(8,128)(2,1)S(1)} fusion(bf16[8192,128]{1,0:T(8,128)(2,1)S(1)} %copy-done, s32[4096]{0:T(1024)S(1)} %broadcast_clamp_fusion), kind=kCustom, calls=%fused_computation | custom fusion | bytes 2113536 | tf_op jit(solution)/shard_map/jit(_take)/gather | solution.py:96
  427.1 197.9 %all-reduce.6.cloned.1.call-done = f32[32,64,128]{2,0,1:T(8,128)} async-done(((f32[32,64,128]{2,0,1:T(8,128)}), f32[32,64,128]{2,0,1:T(8,128)}) %all-reduce.6.cloned.1.call-update) | async-done | bytes 1048592 | tf_op jit(solution)/shard_map/psum | solution.py:98
  625.0 4.4 convolution_bitcast_fusion.1
  629.3 1.8 copy.18
  631.1 3.2 reshape.39
  634.3 3.4 copy.19
  637.7 4.7 copy.20
  642.4 0.0 copy-start.5
  642.4 0.0 all-reduce.8.cloned.1.call-update
  642.4 486.8 %all-reduce.8.cloned.1.call-done = f32[512,4,16,4]{2,3,1,0:T(4,128)} async-done(((f32[512,4,16,4]{2,3,1,0:T(4,128)}), f32[512,4,16,4]{2,3,1,0:T(4,128)}) %all-reduce.8.cloned.1.call-update) | async-done | bytes 524304
  1129.2 0.0 copy-done.5
  1129.2 1.3 fusion.8
  (3 shorter events, 0.0 us)
Async XLA Ops:
  6.5 408.4 %copy-start = (bf16[8192,128]{1,0:T(8,128)(2,1)S(1)}, bf16[8192,128]{1,0:T(8,128)(2,1)}, u32[]{:S(2)}) copy-start(bf16[8192,128]{1,0:T(8,128)(2,1)} %param.17) | copy-start | bytes 6291460
  6.5 104.3 %copy-start.1 = (bf16[128,1792]{1,0:T(8,128)(2,1)S(1)}, bf16[128,1792]{1,0:T(8,128)(2,1)}, u32[]{:S(2)}) copy-start(bf16[128,1792]{1,0:T(8,128)(2,1)} %param.12) | copy-start | bytes 1376260
  6.5 106.0 %copy-start.3 = (bf16[1792,128]{1,0:T(8,128)(2,1)S(1)}, bf16[1792,128]{1,0:T(8,128)(2,1)}, u32[]{:S(2)}) copy-start(bf16[1792,128]{1,0:T(8,128)(2,1)} %param.14) | copy-start | bytes 1376260
  6.5 390.3 %all-reduce.10.cloned.1.call-start = ((), (), s32[]{:S(2)}) async-start(), calls=%async_computation.2 | async-start | bytes 2293760 | tf_op jit(solution)/shard_map/psum | solution.py:68
  113.5 511.5 %all-reduce.6.cloned.1.call-start = ((), (), s32[]{:S(2)}) async-start(), calls=%async_computation | async-start | bytes 2097152 | tf_op jit(solution)/shard_map/psum | solution.py:98
  398.2 16.6 %copy-start.4 = (s32[64,64]{1,0:T(8,128)S(1)}, s32[64,64]{1,0:T(8,128)}, u32[]{:S(2)}) copy-start(s32[64,64]{1,0:T(8,128)} %param.18) | copy-start | bytes 49156
  399.8 1.0 copy-start.2
  403.9 1.0 copy-start.2
  408.0 1.0 copy-start.2
  412.2 1.0 copy-start.2
  414.8 714.4 %all-reduce.8.cloned.1.call-start = ((), (), s32[]{:S(2)}) async-start(), calls=%async_computation.1 | async-start | bytes 8388608
  642.4 486.9 %copy-start.5 = (f32[16,4]{0,1:T(4,128)S(1)}, f32[16,4]{0,1:T(4,128)}, u32[]{:S(2)}) copy-start(f32[16,4]{0,1:T(4,128)} %param.19) | copy-start | bytes 772
Sparse Core Ops, SparseCore 0:
  113.6 283.2 all-reduce.9
  414.9 210.0 all-reduce.5
  642.5 486.6 all-reduce.7
where the time goes:
time: 1140 us
  waiting for transfers between devices  968 us (85%)
  blocking collectives  99.8 us (9%)
  local copies, waits for them, and re-layouts  33.6 us (3%)
  matrix products  15.8 us (1%)
  between operations  13.2 us (1%)
    unnamed x4, waiting for transfers between devices  487 us
    psum x1, waiting for transfers between devices, on_device(): lax.psum((gate_part, up_part, neuron_part), ('feature', 'dp'))  283 us
    psum x1, waiting for transfers between devices, on_device(): width_full = lax.psum(width_part, 'tensor')  198 us
    psum x1, blocking collectives, on_device(): lax.psum(jnp.dot(picker, down_encoder, preferred_element_type=jnp.float32...  99.8 us
  transfers between devices with their start and end apart: 3, of which 3 were waited for; matrix products, arithmetic and copies ran while one was open for 1% of the time, Pallas kernels for 0%

commit v1 on v0

--- a/solution.py
+++ b/solution.py
@@ -65,7 +65,9 @@
     )
     gate_part = jnp.dot(mlp_input, gate_weight, preferred_element_type=jnp.float32)
     up_part = jnp.dot(mlp_input, up_weight, preferred_element_type=jnp.float32)
-    gate_pre, up_pre, neuron_grad = lax.psum((gate_part, up_part, neuron_part), ("feature", "dp"))
+    gate_pre, up_pre, neuron_grad = lax.psum(
+        lax.psum((gate_part, up_part, neuron_part), "feature"), "dp"
+    )
     gate_factor, up_factor = factors(gate_pre, up_pre)
     per_block = math.gcd(features, 8)
     grouped_rows = neuron_grad.reshape(features // per_block, per_block, ffblk)

time: 1140 us -> 1010 us (0.89)
  waiting for transfers between devices: 968 us -> 840 us
    psum x1 -> x2, waiting for transfers between devices: 283 us -> 155 us  [the longest x1 80.5 us: on_device(): lax.psum(lax.psum((gate_part, up_part, neuron_part), 'feature'), 'dp')]
    unnamed x4 -> x5, waiting for transfers between devices: 487 us -> 487 us
  transfers between devices with their start and end apart: 3 -> 4, of which waited for: 3 -> 4; matrix products, arithmetic and copies ran while one was open for 1% -> 1% of each run, Pallas kernels for 0% -> 0%
where the time goes in v1:
time: 1010 us
  waiting for transfers between devices  840 us (83%)
  blocking collectives  99.8 us (10%)
  local copies, waits for them, and re-layouts  33.6 us (3%)
  matrix products  15.8 us (2%)
  between operations  13.2 us (1%)
    unnamed x5, waiting for transfers between devices  487 us
    psum x1, waiting for transfers between devices, on_device(): width_full = lax.psum(width_part, 'tensor')  198 us
    psum x1, blocking collectives, on_device(): lax.psum(jnp.dot(picker, down_encoder, preferred_element_type=jnp.float32...  99.8 us
    psum x1, waiting for transfers between devices, on_device(): lax.psum(lax.psum((gate_part, up_part, neuron_part), 'feature'), 'dp')  80.5 us
    psum x1, waiting for transfers between devices, on_device(): lax.psum((gate_part, up_part, neuron_part), 'feature')  74.3 us
  transfers between devices with their start and end apart: 4, of which 4 were waited for; matrix products, arithmetic and copies ran while one was open for 1% of the time, Pallas kernels for 0%

profile of v1, /device:TPU:2, one launch (start us, length us, event | category | flops | bytes accessed | tf_op | source)
XLA Modules:
  0.0 1008.8 jit_solution(5538792770304123222)
XLA Ops:
  6.5 0.0 copy-start
  6.5 0.0 copy-start.1
  6.5 0.0 all-reduce.12.cloned.1.call-start
  6.6 0.8 broadcast_subtract_fusion
  7.4 1.6 fusion.5
  9.0 99.8 %psum.56 = bf16[32,128]{1,0:T(8,128)(2,1)S(1)} all-reduce(f32[32,128]{1,0:T(8,128)S(1)} %fusion.5), channel_id=1, replica_groups=mesh['tensor'=16,'feature'=8,'dp'=4] {'tensor'}, use_global_device_ids=true, to_apply=%region_0.0 | all-reduce | flops 4096 | bytes 24576 | tf_op jit(solution)/shard_map/psum | solution.py:61
  108.8 2.0 fusion.13
  110.8 0.0 copy-done.1
  110.8 1.7 fusion.14
  112.5 0.0 copy-done.3
  112.5 1.0 fusion.15
  113.5 0.0 all-reduce.12.cloned.1.call-update
  113.5 0.0 all-reduce.14.cloned.1.call-start
  113.5 74.3 %all-reduce.12.cloned.1.call-done = (f32[32,1792]{1,0:T(8,128)}, f32[64,1792]{1,0:T(8,128)}, f32[64,1792]{1,0:T(8,128)}) async-done(((f32[32,1792]{1,0:T(8,128)}, f32[64,1792]{1,0:T(8,128)}, f32[64,1792]{1,0:T(8,128)}), (f32[32,1792]{1,0:T(8,128)}, f32[64,1792]{1,0:T(8,128)}, f32[64,1792]{1,0:T(8,128)})) %all-reduce.12.cloned.1.call-update) | async-done | bytes 1146896 | tf_op jit(solution)/shard_map/psum | solution.py:69
  187.8 0.0 all-reduce.14.cloned.1.call-update
  187.9 0.0 all-reduce.8.cloned.1.call-start
  187.9 80.5 %all-reduce.14.cloned.1.call-done = (f32[4,8,1792]{2,1,0:T(8,128)}, f32[64,1792]{1,0:T(8,128)}, f32[64,1792]{1,0:T(8,128)}) async-done(((f32[4,8,1792]{2,1,0:T(8,128)}, f32[64,1792]{1,0:T(8,128)}, f32[64,1792]{1,0:T(8,128)}), (f32[4,8,1792]{2,1,0:T(8,128)}, f32[64,1792]{1,0:T(8,128)}, f32[64,1792]{1,0:T(8,128)})) %all-reduce.14.cloned.1.call-update) | async-done | bytes 1146896 | tf_op jit(solution)/shard_map/psum | solution.py:68
  268.4 1.4 fusion.6
  269.8 0.0 copy-start.4
  269.8 16.5 %while.10 = (s32[]{:T(128)}, f32[4,8,64,128]{3,1,0,2:T(8,128)}, f32[4,8,1792]{2,1,0:T(8,128)}, f32[64,1792]{1,0:T(8,128)S(1)}, bf16[128,1792]{1,0:T(8,128)(2,1)S...) while((s32[]{:T(128)}, f32[4,8,64,128]{3,1,0,2:T(8,128)}, f32[4,8,1792]{2,1,0:T(8,128)}, ...), condition=%wide.region_8.9_spmd, body=%wide.region_7.8_spmd.sunk | while | flops 473497600 | bytes 12493429 | solution.py:94
  269.8 0.8 dynamic-slice_bitcast_fusion.3
  270.7 0.7 multiply_convert_fusion.3
  271.4 0.0 copy-start.2
  271.4 0.6 fusion.37
  272.0 0.4 copy-done.2
  272.4 0.6 convolution_add_fusion.2
  273.1 0.9 copy_dynamic-update-slice_fusion.2
  273.9 0.8 dynamic-slice_bitcast_fusion.3
  274.8 0.7 multiply_convert_fusion.3
  275.5 0.0 copy-start.2
  275.5 0.6 fusion.37
  276.1 0.4 copy-done.2
  276.5 0.6 convolution_add_fusion.2
  277.2 0.9 copy_dynamic-update-slice_fusion.2
  278.0 0.8 dynamic-slice_bitcast_fusion.3
  278.9 0.7 multiply_convert_fusion.3
  279.6 0.0 copy-start.2
  279.6 0.6 fusion.37
  280.3 0.4 copy-done.2
  280.6 0.6 convolution_add_fusion.2
  281.3 0.9 copy_dynamic-update-slice_fusion.2
  282.2 0.8 dynamic-slice_bitcast_fusion.3
  283.0 0.7 multiply_convert_fusion.3
  283.8 0.0 copy-start.2
  283.8 0.6 fusion.37
  284.4 0.4 copy-done.2
  284.8 0.6 convolution_add_fusion.2
  285.4 0.9 copy_dynamic-update-slice_fusion.2
  286.3 0.0 all-reduce.8.cloned.1.call-update
  286.3 0.0 all-reduce.10.cloned.1.call-start
  286.4 0.0 copy-done.4
  286.4 0.1 reshape.43
  286.5 0.0 copy-done
  286.5 12.1 %gather_fusion = bf16[4096,128]{1,0:T(8,128)(2,1)S(1)} fusion(bf16[8192,128]{1,0:T(8,128)(2,1)S(1)} %copy-done, s32[4096]{0:T(1024)S(1)} %broadcast_clamp_fusion), kind=kCustom, calls=%fused_computation | custom fusion | bytes 2113536 | tf_op jit(solution)/shard_map/jit(_take)/gather | solution.py:98
  298.7 198.1 %all-reduce.8.cloned.1.call-done = f32[32,64,128]{2,0,1:T(8,128)} async-done(((f32[32,64,128]{2,0,1:T(8,128)}), f32[32,64,128]{2,0,1:T(8,128)}) %all-reduce.8.cloned.1.call-update) | async-done | bytes 1048592 | tf_op jit(solution)/shard_map/psum | solution.py:100
  496.7 4.4 convolution_bitcast_fusion
  501.1 1.8 copy.18
  502.9 3.2 reshape.39
  506.1 3.4 copy.19
  509.4 4.7 copy.20
  514.1 0.0 all-reduce.10.cloned.1.call-update
  514.1 486.8 %all-reduce.10.cloned.1.call-done = f32[512,4,16,4]{2,3,1,0:T(4,128)} async-done(((f32[512,4,16,4]{2,3,1,0:T(4,128)}), f32[512,4,16,4]{2,3,1,0:T(4,128)}) %all-reduce.10.cloned.1.call-update) | async-done | bytes 524304
  1000.9 0.0 copy-done.5
  1000.9 1.3 fusion.8
  (5 shorter events, 0.0 us)
Async XLA Ops:
  6.5 280.0 %copy-start = (bf16[8192,128]{1,0:T(8,128)(2,1)S(1)}, bf16[8192,128]{1,0:T(8,128)(2,1)}, u32[]{:S(2)}) copy-start(bf16[8192,128]{1,0:T(8,128)(2,1)} %param.17) | copy-start | bytes 6291460
  6.5 104.3 %copy-start.1 = (bf16[128,1792]{1,0:T(8,128)(2,1)S(1)}, bf16[128,1792]{1,0:T(8,128)(2,1)}, u32[]{:S(2)}) copy-start(bf16[128,1792]{1,0:T(8,128)(2,1)} %param.12) | copy-start | bytes 1376260
  6.5 105.9 %copy-start.3 = (bf16[1792,128]{1,0:T(8,128)(2,1)S(1)}, bf16[1792,128]{1,0:T(8,128)(2,1)}, u32[]{:S(2)}) copy-start(bf16[1792,128]{1,0:T(8,128)(2,1)} %param.14) | copy-start | bytes 1376260
  6.5 181.3 %all-reduce.12.cloned.1.call-start = ((), (), s32[]{:S(2)}) async-start(), calls=%async_computation.2 | async-start | bytes 2293760 | tf_op jit(solution)/shard_map/psum | solution.py:69
  113.5 155.0 %all-reduce.14.cloned.1.call-start = ((), (), s32[]{:S(2)}) async-start(), calls=%async_computation.3 | async-start | bytes 2293760 | tf_op jit(solution)/shard_map/psum | solution.py:68
  187.9 308.9 %all-reduce.8.cloned.1.call-start = ((), (), s32[]{:S(2)}) async-start(), calls=%async_computation | async-start | bytes 2097152 | tf_op jit(solution)/shard_map/psum | solution.py:100
  269.8 16.6 %copy-start.4 = (s32[64,64]{1,0:T(8,128)S(1)}, s32[64,64]{1,0:T(8,128)}, u32[]{:S(2)}) copy-start(s32[64,64]{1,0:T(8,128)} %param.18) | copy-start | bytes 49156
  271.4 1.0 copy-start.2
  275.5 1.0 copy-start.2
  279.6 1.0 copy-start.2
  283.8 1.0 copy-start.2
  286.3 714.6 %all-reduce.10.cloned.1.call-start = ((), (), s32[]{:S(2)}) async-start(), calls=%async_computation.1 | async-start | bytes 8388608
  514.1 486.8 %copy-start.5 = (f32[16,4]{0,1:T(4,128)S(1)}, f32[16,4]{0,1:T(4,128)}, u32[]{:S(2)}) copy-start(f32[16,4]{0,1:T(4,128)} %param.19) | copy-start | bytes 772
Sparse Core Ops, SparseCore 0:
  113.6 74.1 all-reduce.11
  191.0 77.3 all-reduce.13
  286.5 210.2 all-reduce.7
  514.3 486.6 all-reduce.9
